TPU v7x, 512 devices: a whole 4x8x8 slice. The times are simulated.
512 devices in a mesh: member: 16 (over z, x_hi), lat: 32 (over x_lo, y, core).
Axes of the slice: x: 4 (x_hi: 2, x_lo: 2; x = x_hi * 2 + x_lo), y: 8, z: 8, core: 2. Of those that a mesh axis runs over, the one named last changes fastest.
Arguments:
- state: bfloat16 [16, 64, 2, 256, 1024], P('member', None, None, 'lat'), may hold values from -6 to 6
- target: bfloat16 [2, 64, 256, 256], P(None, None, 'lat'), may hold values from -6 to 6
- w_in: bfloat16 [64, 256], replicated, may hold values from -0.75 to 0.75
- w_out: bfloat16 [256, 64], replicated, may hold values from -0.375 to 0.375
- legendre: bfloat16 [256, 256, 256], P('lat'), may hold values from -0.25 to 0.25
- wavenumber_of: int32 [256], replicated, may hold values from 0 to 255, each once
Outputs:
- loss_mean: float32 [], replicated
- grad_w_in: float32 [64, 256], replicated
- grad_w_out: float32 [256, 64], replicated
Inputs may be any that keep to these rules, and one draw needn't show every extreme that they name: `wavenumber_of`: a permutation of the wavenumbers 0 to 256 - 1 over the slots.
All inputs are finite; a program needn't handle non-finite values.
Results may differ from a plain program's by a relative error of at most 0.0055.
Values may be sent and summed in bfloat16 or wider, within the bound.
A program may use at most 64 MiB of HBM per device.

v0:
```python
import math

import jax
import jax.numpy as jnp
from jax import lax
from jax.sharding import PartitionSpec as P


def partner(block, axis, apart):
    count = lax.axis_size(axis)
    route = []
    for low in range(count):
        high = low | 1 << apart
        if high != low and high < count:
            route += [(low, high), (high, low)]
    return lax.ppermute(block, axis, route)


def make_waves(longitude_count, wavenumber_of, slot_count, lane_count):
    slot_waves = wavenumber_of.reshape(lane_count, 1, slot_count)
    col_waves = jnp.broadcast_to(slot_waves, (lane_count, 2, slot_count)).reshape(-1)
    col_part = jnp.broadcast_to(
        jnp.arange(2, dtype=jnp.int32).reshape(1, 2, 1), (lane_count, 2, slot_count)
    ).reshape(-1)
    longitude_cells = jnp.arange(longitude_count, dtype=jnp.int32)
    phase_index = longitude_cells[:, None] * col_waves[None, :] % longitude_count
    angle_rad = phase_index.astype(jnp.float32) * (2.0 * math.pi / longitude_count)
    values = jnp.where(col_part[None, :] == 0, jnp.cos(angle_rad), -jnp.sin(angle_rad)) / math.sqrt(
        longitude_count
    )
    return values.astype(jnp.bfloat16)


def smooth_abs(delta):
    return jnp.sqrt(delta * delta + 1.0) - 1.0


def smooth_slope(delta):
    return delta / jnp.sqrt(delta * delta + 1.0)


def silu_grad(pre_act):
    sigma_value = jax.nn.sigmoid(pre_act)
    return sigma_value * (1.0 + pre_act * (1.0 - sigma_value))


def legendre_forward(fourier_modes, legendre, sign_south, live_mask):
    channels, hemi_count, half_rows, col_count = fourier_modes.shape
    slot_count = legendre.shape[0]
    split_cols = fourier_modes.reshape(channels, hemi_count, half_rows, 2, slot_count)
    hemi_sums = jnp.einsum(
        "chiqs,sni->hqcsn", split_cols, legendre, preferred_element_type=jnp.float32
    )
    return ((hemi_sums[0] + sign_south * hemi_sums[1]) * live_mask).astype(jnp.bfloat16)


def body(state, target, w_in, w_out, legendre, wavenumber_of):
    lane_count = lax.axis_size("lat")
    channels, band_rows, longitude_count = (state.shape[1], state.shape[3], state.shape[4])
    slot_count, degrees = (legendre.shape[0], legendre.shape[1])
    groups = lax.axis_size("member") // 2
    obj_scale = 1.0 / (groups * channels)
    grid_rows = state[0].reshape(channels, -1, longitude_count).transpose(1, 0, 2)

    def network_row(row_field):
        pre_row = jnp.einsum("ck,cx->kx", w_in, row_field, preferred_element_type=jnp.float32)
        hidden_row = jax.nn.silu(pre_row).astype(jnp.bfloat16)
        tendency_row = jnp.einsum(
            "kc,kx->cx", w_out, hidden_row, preferred_element_type=jnp.float32
        )
        return (row_field.astype(jnp.float32) + tendency_row).astype(jnp.bfloat16)

    predicted_rows = lax.map(network_row, grid_rows)
    predicted_field = predicted_rows.transpose(1, 0, 2)
    wavenumber_lookup = make_waves(longitude_count, wavenumber_of, slot_count, lane_count)
    fourier_modes = jnp.dot(
        predicted_field.reshape(-1, longitude_count),
        wavenumber_lookup,
        preferred_element_type=jnp.float32,
    )
    fourier_modes = fourier_modes.astype(jnp.bfloat16).reshape(channels, 2, band_rows, -1)
    by_owner = lax.all_to_all(fourier_modes, "lat", split_axis=3, concat_axis=2, tiled=True)
    slot_start = lax.axis_index("lat") * slot_count
    own_waves = lax.dynamic_slice_in_dim(wavenumber_of, slot_start, slot_count)
    degree = jnp.arange(degrees, dtype=jnp.int32)
    degree_gap = degree[None, :] - own_waves[:, None]
    live_mask = (degree_gap >= 0).astype(jnp.float32)
    sign_south = (1 - 2 * (degree_gap % 2)).astype(jnp.float32)
    coeffs = legendre_forward(by_owner, legendre, sign_south, live_mask)
    mate_coeffs = partner(coeffs, "member", 0)
    own_values = coeffs.astype(jnp.float32)
    misfit = own_values - target.astype(jnp.float32)
    spread = own_values - mate_coeffs.astype(jnp.float32)
    share_part = jnp.sum(live_mask * (0.5 * smooth_abs(misfit) - 0.25 * smooth_abs(spread)))
    coef_grad = (
        live_mask * (0.5 * smooth_slope(misfit) - 0.5 * smooth_slope(spread)) * obj_scale
    ).astype(jnp.bfloat16)
    south_grad = coef_grad * sign_south.astype(jnp.bfloat16)
    stacked = jnp.stack([coef_grad, south_grad])
    back_fourier = jnp.einsum(
        "hqcsn,sni->chiqs", stacked, legendre, preferred_element_type=jnp.float32
    )
    back_fourier = back_fourier.astype(jnp.bfloat16).reshape(channels, 2, -1, 2 * slot_count)
    piece_rows = lax.all_to_all(back_fourier, "lat", split_axis=2, concat_axis=3, tiled=True)
    row_count = piece_rows.shape[0]
    grid_part = jnp.einsum(
        "rj,xj->rx",
        piece_rows.reshape(-1, piece_rows.shape[3]),
        wavenumber_lookup,
        preferred_element_type=jnp.float32,
    )
    grid_grad = grid_part.astype(jnp.bfloat16).reshape(row_count, 2, -1, longitude_count)
    grad_rows = grid_grad.reshape(channels, -1, longitude_count).transpose(1, 0, 2)

    def backward_row(carry, pair):
        acc_in, acc_out = carry
        row_field, row_grad = pair
        pre_row = jnp.einsum("ck,cx->kx", w_in, row_field, preferred_element_type=jnp.float32)
        hidden_row = jax.nn.silu(pre_row).astype(jnp.bfloat16)
        acc_out = acc_out + jnp.einsum(
            "kx,cx->kc", hidden_row, row_grad, preferred_element_type=jnp.float32
        )
        pull_row = jnp.einsum("kc,cx->kx", w_out, row_grad, preferred_element_type=jnp.float32)
        act_row = (pull_row * silu_grad(pre_row)).astype(jnp.bfloat16)
        acc_in = acc_in + jnp.einsum(
            "cx,kx->ck", row_field, act_row, preferred_element_type=jnp.float32
        )
        return ((acc_in, acc_out), None)

    start_in = jnp.zeros(w_in.shape, jnp.float32)
    start_out = jnp.zeros(w_out.shape, jnp.float32)
    (grad_in, grad_out), unused = lax.scan(
        backward_row, (start_in, start_out), (grid_rows, grad_rows)
    )
    grad_in, grad_out, total = lax.psum((grad_in, grad_out, share_part), ("member", "lat"))
    loss_mean = total * obj_scale / (slot_count * lane_count * degrees)
    return (loss_mean, grad_in, grad_out)


def solution(mesh):
    return jax.shard_map(
        body,
        mesh=mesh,
        in_specs=(
            P("member", None, None, "lat", None),
            P(None, None, "lat", None),
            P(),
            P(),
            P("lat", None, None),
            P(),
        ),
        out_specs=(P(), P(), P()),
        check_vma=False,
    )
```

profile of v0, /device:TPU:1, one launch (start us, length us, event | category | flops | bytes accessed | tf_op | source)
XLA Modules:
  0.0 570.9 jit_solution(16295555227650953248)
XLA Ops:
  8.3 2.8 copy.51
  11.1 20.1 %while.23 = (s32[]{:T(128)}, bf16[16,64,1024]{2,1,0:T(8,128)(2,1)}, bf16[16,64,1024]{2,1,0:T(8,128)(2,1)S(1)}, bf16[64,256]{1,0:T(8,128)(2,1)S(1)}, bf16[256,64]{0,1:T(8,128)(2,1)S(1)}, /*index=5*/s32[]{:T(128)}) while((s32[]{:T(128)}, bf16[16,64,1024]{2,1,0:T(8,128)(2,1)}, bf16[16,64,1024]{2,1,0:T(8,128)(2,1)S(1)}, ...), condition=%wide.region_1.2_spmd, body=%wide.region_0.1_spmd.sunk | while | flops 68616192 | bytes 459853 | solution.py:73
  11.1 1.3 fusion.96
  17.4 1.3 fusion.96
  27.4 1.3 fusion.96
  28.7 1.3 fusion.96
  31.2 3.5 copy.52
  34.7 11.2 %convolution_convert_fusion.2 = bf16[1024,512]{1,0:T(8,128)(2,1)} fusion(bf16[1024,1024]{1,0:T(8,128)(2,1)S(1)} %bitcast.155, s32[512]{0:T(512)S(1)} %mul.120, pred[512]{0:T(512)(128)(4,1)S(1)} %eq.20), kind=kOutput, calls=%fused_computation.55 | convolution fusion | flops 1083703296 | bytes 3148288 | tf_op jit(solution)/shard_map/dot_general | solution.py:76
  45.9 4.3 copy.53
  50.2 2.3 reshape.105
  52.5 11.1 %all-to-all-start = ((bf16[32,2,8192]{2,1,0:T(2,128)(2,1)}), bf16[32,2,8192]{2,1,0:T(2,128)(2,1)}, u32[]{:S(2)}, u32[]{:S(2)}) async-start(bf16[32,2,8192]{2,1,0:T(2,128)(2,1)} %reshape.105), calls=%async_computation | async-start | bytes 2097152 | tf_op jit(solution)/shard_map/all_to_all | solution.py:82
  63.8 26.3 %all-to-all-done = bf16[32,2,8192]{2,1,0:T(2,128)(2,1)} async-done(((bf16[32,2,8192]{2,1,0:T(2,128)(2,1)}), bf16[32,2,8192]{2,1,0:T(2,128)(2,1)}, u32[]{:S(2)}, u32[]{:S(2)}) %all-to-all-start) | async-done | bytes 1048608 | tf_op jit(solution)/shard_map/all_to_all | solution.py:82
  90.1 3.8 reshape.106
  95.6 3.1 collective-permute-start
  98.7 11.4 %collective-permute-done = bf16[2,64,8,256]{3,1,0,2:T(8,128)(2,1)S(1)} collective-permute-done((bf16[2,64,8,256]{3,1,0,2:T(8,128)(2,1)S(1)}, bf16[2,64,8,256]{3,1,0,2:T(8,128)(2,1)S(1)}, u32[]{:S(2)}, u32[]{:S(2)}) %collective-permute-start) | collective-permute-done | bytes 524320 | tf_op jit(solution)/shard_map/ppermute | solution.py:16
  110.1 1.4 multiply_bitcast_fusion
  112.1 1.6 copy.81
  113.6 5.4 copy.61
  119.0 4.6 reshape.107
  123.6 8.8 %all-to-all-start.1 = ((bf16[32,2,8192]{2,1,0:T(2,128)(2,1)}), bf16[32,2,8192]{2,1,0:T(2,128)(2,1)}, u32[]{:S(2)}, u32[]{:S(2)}) async-start(bf16[32,2,8192]{2,1,0:T(2,128)(2,1)} %reshape.107), calls=%async_computation.1 | async-start | bytes 2097152 | tf_op jit(solution)/shard_map/all_to_all | solution.py:104
  132.6 26.4 %all-to-all-done.1 = bf16[32,2,8192]{2,1,0:T(2,128)(2,1)} async-done(((bf16[32,2,8192]{2,1,0:T(2,128)(2,1)}), bf16[32,2,8192]{2,1,0:T(2,128)(2,1)}, u32[]{:S(2)}, u32[]{:S(2)}) %all-to-all-start.1) | async-done | bytes 1048608 | tf_op jit(solution)/shard_map/all_to_all | solution.py:104
  159.0 4.7 reshape.108
  163.7 13.6 %copy.63 = bf16[64,2,8,32,16]{4,3,2,1,0:T(8,128)(2,1)} copy(bf16[64,2,8,32,16]{0,4,1,2,3:T(8,128)(2,1)} %bitcast.147) | data formatting | bytes 2097152 | tf_op jit(solution)/shard_map/all_to_all | solution.py:104
  177.3 15.1 %reshape.103 = bf16[1024,512]{1,0:T(8,128)(2,1)} reshape(bf16[64,2,8,32,16]{4,3,2,1,0:T(8,128)(2,1)} %copy.63) | data formatting | bytes 2097152 | tf_op jit(solution)/shard_map/reshape | solution.py:108
  192.4 11.3 %convolution_convert_fusion = bf16[1024,1024]{1,0:T(8,128)(2,1)S(1)} fusion(bf16[1024,512]{1,0:T(8,128)(2,1)} %reshape.103, s32[512]{0:T(512)S(1)} %mul.120, pred[512]{0:T(512)(128)(4,1)S(1)} %eq.20), kind=kOutput, calls=%fused_computation.52 | convolution fusion | flops 1084227584 | bytes 3148288 | tf_op jit(solution)/shard_map/rj,xj->rx/dot_general | solution.py:106
  203.7 2.5 copy.80
  206.2 89.2 %while.24 = (s32[]{:T(128)}, f32[64,256]{1,0:T(8,128)S(1)}, f32[256,64]{0,1:T(8,128)S(1)}, bf16[16,64,1024]{2,1,0:T(8,128)(2,1)}, bf16[16,64,1024]{2,1,0:T(8,128...) while((s32[]{:T(128)}, f32[64,256]{1,0:T(8,128)S(1)}, ...), condition=%wide.region_5.6_spmd.clone, body=%wide.region_4.5_spmd.clone.sunk | while | flops 137953280 | bytes 8193683 | solution.py:132
  208.4 1.3 convolution_add_fusion.2
  209.7 2.0 fusion.103
  214.0 1.3 convolution_add_fusion.2
  215.3 2.0 fusion.103
  219.5 1.3 convolution_add_fusion.2
  220.9 2.0 fusion.103
  225.1 1.3 convolution_add_fusion.2
  226.5 2.0 fusion.103
  230.7 1.3 convolution_add_fusion.2
  232.0 2.0 fusion.103
  236.3 1.3 convolution_add_fusion.2
  237.6 2.0 fusion.103
  241.9 1.3 convolution_add_fusion.2
  243.2 2.0 fusion.103
  247.4 1.3 convolution_add_fusion.2
  248.8 2.0 fusion.103
  253.0 1.3 convolution_add_fusion.2
  254.4 2.0 fusion.103
  258.6 1.3 convolution_add_fusion.2
  259.9 2.0 fusion.103
  264.2 1.3 convolution_add_fusion.2
  265.5 2.0 fusion.103
  269.7 1.3 convolution_add_fusion.2
  271.1 2.0 fusion.103
  275.3 1.3 convolution_add_fusion.2
  276.7 2.0 fusion.103
  280.9 1.3 convolution_add_fusion.2
  282.3 2.0 fusion.103
  286.5 1.3 convolution_add_fusion.2
  287.8 2.0 fusion.103
  292.1 1.3 convolution_add_fusion.2
  293.4 2.0 fusion.103
  296.1 2.9 multiply_reduce_fusion
  299.0 104.3 %psum.21 = f32[]{:T(128)} all-reduce(f32[]{:T(128)} %multiply_reduce_fusion), channel_id=1, replica_groups=mesh['member'=16,'lat'=32] {'member','lat'}, use_global_device_ids=true, to_apply=%region_3.4 | all-reduce | flops 1 | bytes 8 | tf_op jit(solution)/shard_map/psum | solution.py:135
  403.9 156.1 %all-reduce.3.cloned.1.call-done = (f32[64,256]{1,0:T(8,128)}, f32[256,64]{0,1:T(8,128)}) async-done(((f32[64,256]{1,0:T(8,128)}, f32[256,64]{0,1:T(8,128)}), (f32[64,256]{1,0:T(8,128)}, f32[256,64]{0,1:T(8,128)})) %all-reduce.3.cloned.1.call-update) | async-done | bytes 131088 | tf_op jit(solution)/shard_map/psum | solution.py:135
  560.0 1.5 copy.100
  561.5 1.5 copy.101
  (95 shorter events, 54.3 us)
Async XLA Ops:
  7.2 87.3 %copy-start = (bf16[8,256,256]{2,1,0:T(8,128)(2,1)S(1)}, bf16[8,256,256]{2,1,0:T(8,128)(2,1)}, u32[]{:S(2)}) copy-start(bf16[8,256,256]{2,1,0:T(8,128)(2,1)} %param.14) | copy-start | bytes 3145732
  8.3 2.8 copy-start.5
  8.3 2.8 copy-start.9
  31.2 3.5 copy-start.2
  50.2 13.4 %copy-start.8 = (s32[256]{0:T(256)S(1)}, s32[256]{0:T(256)}, u32[]{:S(2)}) copy-start(s32[256]{0:T(256)} %param.15) | copy-start | bytes 3076
  52.5 37.7 %all-to-all-start = ((bf16[32,2,8192]{2,1,0:T(2,128)(2,1)}), bf16[32,2,8192]{2,1,0:T(2,128)(2,1)}, u32[]{:S(2)}, u32[]{:S(2)}) async-start(bf16[32,2,8192]{2,1,0:T(2,128)(2,1)} %reshape.105), calls=%async_computation | async-start | bytes 2097152 | tf_op jit(solution)/shard_map/all_to_all | solution.py:82
  95.3 14.8 %copy-start.3 = (bf16[2,64,8,256]{3,2,1,0:T(8,128)(2,1)S(1)}, bf16[2,64,8,256]{3,2,1,0:T(8,128)(2,1)}, u32[]{:S(2)}) copy-start(bf16[2,64,8,256]{3,2,1,0:T(8,128)(2,1)} %param.11) | copy-start | bytes 1572868
  95.6 14.6 %collective-permute-start = (bf16[2,64,8,256]{3,1,0,2:T(8,128)(2,1)S(1)}, bf16[2,64,8,256]{3,1,0,2:T(8,128)(2,1)S(1)}, u32[]{:S(2)}, u32[]{:S(2)}) collective-permute-start(bf16[2,64,8,256]{3,1,0,2:T(8,128)(2,1)S(1)} %fusion.52), channel_id=1, source_target_pairs={{0,32},{32,0},{64,96},{96,64},{128,160},{160,128},{192,224},{224,1... | collective-permute-start | bytes 1572872 | tf_op jit(solution)/shard_map/ppermute | solution.py:16
  110.1 1.5 copy-start.4
  123.6 35.4 %all-to-all-start.1 = ((bf16[32,2,8192]{2,1,0:T(2,128)(2,1)}), bf16[32,2,8192]{2,1,0:T(2,128)(2,1)}, u32[]{:S(2)}, u32[]{:S(2)}) async-start(bf16[32,2,8192]{2,1,0:T(2,128)(2,1)} %reshape.107), calls=%async_computation.1 | async-start | bytes 2097152 | tf_op jit(solution)/shard_map/all_to_all | solution.py:104
  132.5 427.5 %all-reduce.3.cloned.1.call-start = ((), (), s32[]{:S(2)}) async-start(), calls=%async_computation.2 | async-start | bytes 262144 | tf_op jit(solution)/shard_map/psum | solution.py:135
  207.4 1.0 copy-start.1
  213.0 1.0 copy-start.1
  218.6 1.0 copy-start.1
  224.1 1.0 copy-start.1
  229.7 1.0 copy-start.1
  235.3 1.0 copy-start.1
  240.9 1.0 copy-start.1
  246.5 1.0 copy-start.1
  252.0 1.0 copy-start.1
  257.6 1.0 copy-start.1
  263.2 1.0 copy-start.1
  268.8 1.0 copy-start.1
  274.4 1.0 copy-start.1
  279.9 1.0 copy-start.1
  285.5 1.0 copy-start.1
  291.1 1.0 copy-start.1
  295.4 0.6 copy-start.6
  295.4 0.6 copy-start.7
Sparse Core Ops, SparseCore 0:
  296.2 263.7 all-reduce.2
where the time goes:
time: 573 us; the launch traced here: 571 us
  waiting for transfers between devices  220 us (38%)
  matrix products  117 us (20%)
  blocking collectives  104 us (18%)
  local copies, waits for them, and re-layouts  84.7 us (15%)
  starting transfers between devices  23.1 us (4%)
  between operations  16.1 us (3%)
    psum x1, waiting for transfers between devices, body(): lax.psum((grad_in, grad_out, share_part), ('member', 'lat'))  156 us
    psum x1, blocking collectives, body(): lax.psum((grad_in, grad_out, share_part), ('member', 'lat'))  104 us
    dot_general x16, matrix products, backward_row(): jnp.einsum('cx,kx->ck', row_field, act_row, preferred_element_type=jnp.fl...  31.9 us
    all_to_all x1, waiting for transfers between devices, body(): lax.all_to_all(back_fourier, 'lat', split_axis=2, concat_axis=3, tiled=True)  26.4 us
    all_to_all x1, waiting for transfers between devices, body(): lax.all_to_all(fourier_modes, 'lat', split_axis=3, concat_axis=2, tiled=T...  26.3 us
    unnamed x25, local copies, waits for them, and re-layouts  21.7 us
    dot_general x16, matrix products, backward_row(): jnp.einsum('kx,cx->kc', hidden_row, row_grad, preferred_element_type=jnp....  21.4 us
    dot_general x16, matrix products, network_row(): jnp.einsum('kc,kx->cx', w_out, hidden_row, preferred_element_type=jnp.flo...  20.1 us
  transfers between devices with their start and end apart: 4, of which 4 were waited for; matrix products, arithmetic and copies ran while one was open for 1% of the time, Pallas kernels for 0%

commit v1 on v0

v1 whole, which is shorter than its diff:
```python
import functools
import math

import jax
import jax.numpy as jnp
import numpy as np
from jax import lax
from jax.experimental import pallas as pl
from jax.experimental.pallas import tpu as pltpu
from jax.sharding import PartitionSpec as P

MESH = pl.DeviceIdType.MESH
F32 = jnp.float32
BF16 = jnp.bfloat16
XC = 256
JP = 4


def dot(a, b):
    return jnp.dot(a, b, preferred_element_type=F32)


def base_table(nlon, waves):
    cell = np.arange(nlon, dtype=np.int64)[None, :]
    wave = np.arange(waves, dtype=np.int64)[:, None]
    angle = (cell * wave % nlon).astype(np.float32) * np.float32(2.0 * math.pi / nlon)
    both = np.concatenate([np.cos(angle), -np.sin(angle)], axis=0) / np.float32(math.sqrt(nlon))
    return both.astype(jnp.bfloat16)


def kernel(
    nm, nl, state_hbm, target_hbm, w_in_ref, w_out_ref, leg_hbm, base_hbm, wcol_ref,
    out_in, out_out, out_loss,
    st_raw, st32, s_cx, base, wave_t, wave, w_in_bd, w_out_bd, w_pull, hid, slope, fore,
    sf, rf, rf32, fg32, sg, rg, leg, leg_t, tgt, tw, tgt_t, acc32, gb, bs, acc,
    lsend, lrow1, lsend2, lrow2, ar_s, ar_a, ar_p, ar_b, ar_q, ar_c,
    in_sem, send1, recv1, send2, recv2, ls_sem, lr_sem, as_sem, arr_sem,
):
    member = lax.axis_index("member")
    lat = lax.axis_index("lat")
    half = lax.rem(member, 2)
    base_member = member - half
    ng = 2 * nl
    me = half * nl + lat
    nlon = wave.shape[0]
    cols = wave.shape[1]
    waves = cols // 2
    deg = leg.shape[1]
    nj = leg.shape[2]

    def at64(t):
        return (base_member + t // nl, lax.rem(t, nl))

    c_state = pltpu.make_async_copy(state_hbm, st_raw, in_sem.at[0])
    c_base = pltpu.make_async_copy(base_hbm, base, in_sem.at[1])
    c_leg = pltpu.make_async_copy(leg_hbm.at[pl.ds(half * 4, 4)], leg, in_sem.at[2])
    c_tgt = pltpu.make_async_copy(target_hbm, tgt, in_sem.at[3])
    c_state.start()
    c_base.start()
    c_leg.start()
    c_tgt.start()

    barrier = pltpu.get_barrier_semaphore()

    def greet(d, carry):
        pl.semaphore_signal(barrier, inc=1, device_id=at64(lax.rem(me + d, ng)), device_id_type=MESH)
        return carry

    lax.fori_loop(1, ng, greet, 0)

    def greet_member(d, carry):
        other = lax.rem(base_member + d, nm)
        pl.semaphore_signal(barrier, inc=1, device_id=(other, lat), device_id_type=MESH)
        return carry

    lax.fori_loop(2, nm, greet_member, 0)

    w_in_bd[...] = jnp.zeros_like(w_in_bd)
    w_pull[...] = jnp.zeros_like(w_pull)
    wide = w_out_ref[...].astype(F32)
    wide = jnp.concatenate([wide, wide, wide, wide], axis=1)
    wide_t = wide.T.astype(BF16)
    lane_group = lax.broadcasted_iota(jnp.int32, wide.shape, 1) >> 6
    for g in range(4):
        w_in_bd[64 * g : 64 * g + 64, 256 * g : 256 * g + 256] = w_in_ref[...]
        w_pull[64 * g : 64 * g + 64, 256 * g : 256 * g + 256] = wide_t[64 * g : 64 * g + 64]
        w_out_bd[256 * g : 256 * g + 256, :] = jnp.where(lane_group == g, wide, 0.0).astype(BF16)

    c_state.wait()

    def widen(xt, carry):
        lanes = pl.ds(pl.multiple_of(xt * 128, 128), 128)
        st32[xt] = st_raw[:, :, :, lanes].astype(F32).reshape(st32.shape[1], 128)
        return carry

    lax.fori_loop(0, nlon // 128, widen, 0)

    c_base.wait()
    lb = min(128, waves)
    rb = min(128, cols)

    def order_rows(r, carry):
        rows = pl.ds(pl.multiple_of(r * rb, rb), rb)
        wcol = wcol_ref[rows, :][:, :lb]
        part = (lax.broadcasted_iota(jnp.int32, (rb, lb), 0) >> 2) & 1
        lane = lax.broadcasted_iota(jnp.int32, (rb, lb), 1)
        blocks = []
        for b in range(cols // lb):
            q, first = b * lb // waves, b * lb % waves
            hit = jnp.where(wcol == lane + first, 1.0, 0.0) * jnp.where(part == q, 1.0, 0.0)
            blocks.append(hit)
        pick = jnp.concatenate(blocks, axis=1).astype(BF16)
        wave_t[rows, :] = dot(pick, base[...]).astype(BF16)
        return carry

    lax.fori_loop(0, cols // rb, order_rows, 0)

    def send_chunk(jp, src, dst, ssem, rsem):
        def one(d, carry):
            t = lax.rem(me + d, ng)
            pltpu.make_async_remote_copy(
                src_ref=src.at[jp, t], dst_ref=dst.at[jp, me],
                send_sem=ssem.at[jp], recv_sem=rsem.at[jp],
                device_id=at64(t), device_id_type=MESH,
            ).start()
            return carry

        lax.fori_loop(1, ng, one, 0)

    def wait_bytes(ref, sem):
        pltpu.make_async_copy(ref, ref, sem).wait()

    def forward(jp, carry):
        def network(xc, inner):
            rows = pl.ds(pl.multiple_of(xc * XC, XC), XC)
            turned = []
            for xt in range(XC // 128):
                tile = xc * (XC // 128) + xt
                parts = [
                    st32[tile, pl.ds(h * 8 + jp * 2 + j2, 64, stride=16), :]
                    for j2 in range(2) for h in range(2)
                ]
                block = jnp.concatenate(parts, axis=0)
                s_cx[jp, :, pl.ds(pl.multiple_of(tile * 128, 128), 128)] = block.astype(BF16)
                turned.append(block.T)
            field = jnp.concatenate(turned, axis=0)
            pre = dot(field.astype(BF16), w_in_bd[...])
            sig = 0.5 + 0.5 * jnp.tanh(0.5 * pre)
            hidden = (pre * sig).astype(BF16)
            hid[jp, rows, :] = hidden
            slope[jp, rows, :] = (sig * (1.0 + pre * (1.0 - sig))).astype(BF16)
            fore[rows, :] = (field + dot(hidden, w_out_bd[...])).astype(BF16)
            return inner

        lax.fori_loop(0, nlon // XC, network, 0)
        modes = dot(wave_t[...], fore[...])
        pair = [modes[:, :128].reshape(ng, 8, 128), modes[:, 128:].reshape(ng, 8, 128)]
        sf[jp] = jnp.concatenate(pair, axis=1).astype(BF16)

        @pl.when(jp == 0)
        def _():
            pl.semaphore_wait(barrier, ng - 1 + nm - 2)

        send_chunk(jp, sf, rf, send1, recv1)
        rf[jp, me] = sf[jp, me]
        return carry

    lax.fori_loop(0, JP, forward, 0)

    def turn_wave(xt, carry):
        start = pl.multiple_of(xt * 128, 128)
        wave[pl.ds(start, 128), :] = wave_t[:, pl.ds(start, 128)].astype(F32).T.astype(BF16)
        return carry

    lax.fori_loop(0, nlon // 128, turn_wave, 0)
    c_leg.wait()
    c_tgt.wait()
    for i in range(4):
        leg_t[i] = leg[i].astype(F32).T.astype(BF16)
    for b in range(deg // 128):
        tw[b] = tgt[:, :, :, 128 * b : 128 * b + 128].astype(F32).reshape(tw.shape[1], 128)
    for b in range(deg // 128):
        for i in range(8):
            parts = [tw[b, pl.ds(q * 512 + i, 64, stride=8), :] for q in (0, 0, 1, 1)]
            tgt_t[i, 128 * b : 128 * b + 128, :] = jnp.concatenate(parts, axis=0).T.astype(BF16)

    def arrived(jp, carry):
        wait_bytes(rf.at[jp, pl.ds(0, ng - 1)], recv1.at[jp])
        rf32[:, pl.ds(pl.multiple_of(jp * 16, 16), 16), :] = rf[jp].astype(F32)
        return carry

    lax.fori_loop(0, JP, arrived, 0)

    for i in range(4):
        for e in range(2):
            parts = [
                rf32[e * nl : e * nl + nl, pl.ds(q * 4 + i, 8, stride=8), :].reshape(nj, 128)
                for q in range(2)
            ]
            acc32[i, e] = dot(leg[i], jnp.concatenate(parts, axis=1).astype(BF16))

    own = wcol_ref[pl.ds(pl.multiple_of(me * 8, 8), 8), :]
    obj = 1.0 / ((nm // 2) * 64)
    nb = 64

    def compare(c, carry):
        rows = pl.ds(pl.multiple_of(c * nb, nb), nb)
        degree = lax.broadcasted_iota(jnp.int32, (nb, 128), 0) + c * nb
        south = lax.broadcasted_iota(jnp.int32, (nb, 128), 1) >= 64
        loss = jnp.zeros((nb, 128), F32)
        for i in range(4):
            gap = degree - own[i : i + 1, :]
            live = gap >= 0
            sign = jnp.where((gap & 1) == 0, 1.0, -1.0)
            turn = jnp.where(south, sign, 1.0)
            for q in range(2):
                lanes = slice(128 * q, 128 * q + 128)
                coeffs = []
                for e in range(2):
                    part = acc32[i, e, rows, lanes]
                    whole = part + sign * pltpu.roll(part, 64, axis=1)
                    coeffs.append(jnp.where(live, whole, 0.0).astype(BF16).astype(F32))
                aim = tgt_t[half * 4 + i, rows, lanes].astype(F32) * turn
                d0, d1, ds = coeffs[0] - aim, coeffs[1] - aim, coeffs[0] - coeffs[1]
                u0, u1, us = d0 * d0 + 1.0, d1 * d1 + 1.0, ds * ds + 1.0
                r0, r1, rs = lax.rsqrt(u0), lax.rsqrt(u1), lax.rsqrt(us)
                term = 0.5 * ((u0 * r0 - 1.0) + (u1 * r1 - 1.0) - (us * rs - 1.0))
                loss = loss + jnp.where(live, term, 0.0)
                slope_s = 0.5 * (ds * rs)
                gb[i, 0, rows, lanes] = jnp.where(live, (0.5 * (d0 * r0) - slope_s) * obj, 0.0).astype(BF16)
                gb[i, 1, rows, lanes] = jnp.where(live, (0.5 * (d1 * r1) + slope_s) * obj, 0.0).astype(BF16)
        return carry + jnp.sum(loss.reshape(nb // 8, 8, 128), axis=0)

    loss8 = lax.fori_loop(0, deg // nb, compare, jnp.zeros((8, 128), F32))

    for i in range(4):
        for e in range(2):
            back = dot(leg_t[i], gb[i, e])
            for q in range(2):
                fg32[e * nl : e * nl + nl, pl.ds(q * 4 + i, 8, stride=8), :] = back[
                    :, 128 * q : 128 * q + 128
                ].reshape(nl, 8, 128)

    def give_back(jp, carry):
        sg[jp] = fg32[:, pl.ds(pl.multiple_of(jp * 16, 16), 16), :].astype(BF16)
        send_chunk(jp, sg, rg, send2, recv2)
        rg[jp, me] = sg[jp, me]
        return carry

    lax.fori_loop(0, JP, give_back, 0)

    def to_lats(src_of, dst, ssem, rsem):
        def one(d, carry):
            t = lax.rem(lat + d, nl)
            pltpu.make_async_remote_copy(
                src_ref=src_of(t), dst_ref=dst.at[lat], send_sem=ssem, recv_sem=rsem,
                device_id=(member, t), device_id_type=MESH,
            ).start()
            return carry

        lax.fori_loop(1, nl, one, 0)

    def to_members(src, dst, ssem, rsem):
        def one(d, carry):
            t = lax.rem(member + d, nm)
            pltpu.make_async_remote_copy(
                src_ref=src, dst_ref=dst.at[member], send_sem=ssem, recv_sem=rsem,
                device_id=(t, lat), device_id_type=MESH,
            ).start()
            return carry

        lax.fori_loop(1, nm, one, 0)

    lsend[...] = jnp.sum(loss8, axis=0, keepdims=True)
    to_lats(lambda t: lsend, lrow1, ls_sem.at[0], lr_sem.at[0])
    lrow1[lat] = lsend[...]

    acc[...] = jnp.zeros_like(acc)

    def backward(jp, carry):
        wait_bytes(rg.at[jp, pl.ds(0, ng - 1)], recv2.at[jp])
        block = rg[jp].astype(F32)
        bs[:, :128] = block[:, :8].reshape(cols, 128).astype(BF16)
        bs[:, 128:] = block[:, 8:].reshape(cols, 128).astype(BF16)

        def network(xc, inner):
            rows = pl.ds(pl.multiple_of(xc * XC, XC), XC)
            grad = dot(wave[rows, :], bs[...]).astype(BF16)
            act = (dot(grad, w_pull[...]) * slope[jp, rows, :].astype(F32)).astype(BF16)
            turned = grad.astype(F32).T.astype(BF16)
            top = jnp.zeros((64, 256), F32)
            low = jnp.zeros((64, 256), F32)
            for g in range(4):
                lanes = slice(256 * g, 256 * g + 256)
                top = top + dot(turned[64 * g : 64 * g + 64], hid[jp, rows, lanes])
                low = low + dot(s_cx[jp, 64 * g : 64 * g + 64, rows], act[:, lanes])
            acc[:64] += top
            acc[64:] += low
            return inner

        lax.fori_loop(0, nlon // XC, network, 0)
        return carry

    lax.fori_loop(0, 1, backward, 0)
    wait_bytes(lrow1.at[pl.ds(0, nl - 1)], lr_sem.at[0])
    lsend2[...] = jnp.sum(lrow1[...], axis=0)
    to_members(lsend2, lrow2, ls_sem.at[1], lr_sem.at[1])
    lrow2[member] = lsend2[...]
    lax.fori_loop(1, JP, backward, 0)

    per = 32 // nl
    for t in range(32):
        r, c = t // 2, t % 2
        ar_s[t // per, 8 * (t % per) : 8 * (t % per) + 8, :] = acc[8 * r : 8 * r + 8, 128 * c : 128 * c + 128]
    to_lats(lambda t: ar_s.at[t], ar_a, as_sem.at[0], arr_sem.at[0])
    ar_a[lat] = ar_s[lat]
    wait_bytes(ar_a.at[pl.ds(0, nl - 1)], arr_sem.at[0])
    ar_p[...] = jnp.sum(ar_a[...], axis=0)
    to_members(ar_p, ar_b, as_sem.at[1], arr_sem.at[1])
    ar_b[member] = ar_p[...]
    wait_bytes(ar_b.at[pl.ds(0, nm - 1)], arr_sem.at[1])
    ar_q[...] = jnp.sum(ar_b[...], axis=0)
    to_lats(lambda t: ar_q, ar_c, as_sem.at[2], arr_sem.at[2])
    ar_c[lat] = ar_q[...]
    wait_bytes(lrow2.at[pl.ds(0, nm - 1)], lr_sem.at[1])
    out_loss[...] = jnp.sum(lrow2[...], axis=0)
    wait_bytes(ar_c.at[pl.ds(0, nl - 1)], arr_sem.at[2])
    for t in range(32):
        r, c = t // 2, t % 2
        piece = ar_c[t // per, 8 * (t % per) : 8 * (t % per) + 8, :]
        if r < 8:
            out_out[8 * r : 8 * r + 8, 128 * c : 128 * c + 128] = piece
        else:
            out_in[8 * r - 64 : 8 * r - 56, 128 * c : 128 * c + 128] = piece

    def sent(jp, carry):
        wait_bytes(sf.at[jp, pl.ds(0, ng - 1)], send1.at[jp])
        wait_bytes(sg.at[jp, pl.ds(0, ng - 1)], send2.at[jp])
        return carry

    lax.fori_loop(0, JP, sent, 0)
    wait_bytes(lrow1.at[pl.ds(0, nl - 1)], ls_sem.at[0])
    wait_bytes(lrow2.at[pl.ds(0, nm - 1)], ls_sem.at[1])
    wait_bytes(ar_a.at[pl.ds(0, nl - 1)], as_sem.at[0])
    wait_bytes(ar_b.at[pl.ds(0, nm - 1)], as_sem.at[1])
    wait_bytes(ar_c.at[pl.ds(0, nl - 1)], as_sem.at[2])


def body(nm, nl, state, target, w_in, w_out, legendre, wavenumber_of):
    _, channels, hemis, rows, nlon = state.shape
    slots, deg, nj = legendre.shape
    waves = slots * nl
    cols = 2 * waves
    ng = 2 * nl
    base = jnp.asarray(base_table(nlon, waves))
    order = wavenumber_of.reshape(nl, 2, 1, 4).transpose(1, 0, 2, 3)
    order = jnp.broadcast_to(order, (2, nl, 2, 4)).reshape(cols, 1)
    wcol = jnp.broadcast_to(order, (cols, 128))
    vmem = pl.BlockSpec(memory_space=pltpu.VMEM)
    hbm = pl.BlockSpec(memory_space=pl.ANY)
    dma = pltpu.SemaphoreType.DMA
    piece = 8 * (32 // nl)
    v = pltpu.VMEM
    grad_in, grad_out, loss = pl.pallas_call(
        functools.partial(kernel, nm, nl),
        out_shape=(
            jax.ShapeDtypeStruct((64, 256), F32),
            jax.ShapeDtypeStruct((64, 256), F32),
            jax.ShapeDtypeStruct((1, 128), F32),
        ),
        in_specs=[hbm, hbm, vmem, vmem, hbm, hbm, vmem],
        out_specs=(vmem, vmem, vmem),
        scratch_shapes=[
            v((channels, hemis, rows, nlon), BF16),
            v((nlon // 128, channels * hemis * rows, 128), F32),
            v((JP, 256, nlon), BF16),
            v((cols, nlon), BF16),
            v((cols, nlon), BF16),
            v((nlon, cols), BF16),
            v((256, 1024), BF16),
            v((1024, 256), BF16),
            v((256, 1024), BF16),
            v((JP, nlon, 1024), BF16),
            v((JP, nlon, 1024), BF16),
            v((nlon, 256), BF16),
            v((JP, ng, 16, 128), BF16),
            v((JP, ng, 16, 128), BF16),
            v((ng, 64, 128), F32),
            v((ng, 64, 128), F32),
            v((JP, ng, 16, 128), BF16),
            v((JP, ng, 16, 128), BF16),
            v((4, deg, nj), BF16),
            v((4, nj, deg), BF16),
            v((2, channels, slots, deg), BF16),
            v((deg // 128, 2 * channels * slots, 128), F32),
            v((8, deg, 256), BF16),
            v((4, 2, deg, 256), F32),
            v((4, 2, deg, 256), BF16),
            v((cols, 256), BF16),
            v((128, 256), F32),
            v((1, 128), F32),
            v((nl, 1, 128), F32),
            v((1, 128), F32),
            v((nm, 1, 128), F32),
            v((nl, piece, 128), F32),
            v((nl, piece, 128), F32),
            v((piece, 128), F32),
            v((nm, piece, 128), F32),
            v((piece, 128), F32),
            v((nl, piece, 128), F32),
            dma((4,)), dma((JP,)), dma((JP,)), dma((JP,)), dma((JP,)),
            dma((2,)), dma((2,)), dma((3,)), dma((3,)),
        ],
        compiler_params=pltpu.CompilerParams(
            collective_id=0, has_side_effects=True, vmem_limit_bytes=60 * 1024 * 1024
        ),
    )(state[0], target, w_in, w_out, legendre, base, wcol)
    groups = nm // 2
    scale = 0.5 / (groups * channels) / (waves * deg)
    return jnp.sum(loss) * scale, grad_in, grad_out.T


def solution(mesh):
    return jax.shard_map(
        functools.partial(body, mesh.shape["member"], mesh.shape["lat"]),
        mesh=mesh,
        in_specs=(
            P("member", None, None, "lat", None),
            P(None, None, "lat", None),
            P(),
            P(),
            P("lat", None, None),
            P(),
        ),
        out_specs=(P(), P(), P()),
        check_vma=False,
    )
```

time: 573 us -> 114 us (0.20)
  waiting for transfers between devices: 220 us -> 0 us
  matrix products: 117 us -> 0 us
  Pallas kernels: 0 us -> 104 us
  blocking collectives: 104 us -> 0 us
  local copies, waits for them, and re-layouts: 84.7 us -> 6.22 us
  starting transfers between devices: 23.1 us -> 0 us
  between operations: 16.1 us -> 2.45 us
    psum x1 -> x0, waiting for transfers between devices: 156 us -> none  [body(): lax.psum((grad_in, grad_out, share_part), ('member', 'lat'))]
    dot_general x68 -> x0, matrix products: 117 us -> none  [the longest x16 31.9 us: backward_row(): jnp.einsum('cx,kx->ck', row_field, act_row, preferred_element_type=jnp.fl...]
    psum x1 -> x0, blocking collectives: 104 us -> none  [body(): lax.psum((grad_in, grad_out, share_part), ('member', 'lat'))]
    pallas_call x0 -> x1, Pallas kernels: none -> 104 us  [body(): pl.pallas_call(functools.partial(kernel, nm, nl), out_shape=(jax.ShapeDty...]
    all_to_all x2 -> x0, waiting for transfers between devices: 52.7 us -> none  [the longest x1 26.4 us: body(): lax.all_to_all(back_fourier, 'lat', split_axis=2, concat_axis=3, tiled=True)]
    reshape x3 -> x1, local copies, waits for them, and re-layouts: 24.8 us -> 0.8 us  [body(): order = wavenumber_of.reshape(nl, 2, 1, 4).transpose(1, 0, 2, 3)]
    all_to_all x2 -> x0, starting transfers between devices: 20 us -> none  [the longest x1 11.1 us: body(): lax.all_to_all(fourier_modes, 'lat', split_axis=3, concat_axis=2, tiled=T...]
    while x33 -> x0, local copies, waits for them, and re-layouts: 18.9 us -> none
  transfers between devices with their start and end apart: 4 -> 0, of which waited for: 4 -> 0; matrix products, arithmetic and copies ran while one was open for 1% -> 0% of each run, Pallas kernels for 0% -> 0%
where the time goes in v1:
time: 114 us
  Pallas kernels  104 us (91%)
  local copies, waits for them, and re-layouts  6.22 us (5%)
  between operations  2.45 us (2%)
  other arithmetic  1.27 us (1%)
    pallas_call x1, Pallas kernels, body(): pl.pallas_call(functools.partial(kernel, nm, nl), out_shape=(jax.ShapeDty...  104 us
    unnamed x3, local copies, waits for them, and re-layouts  4.44 us

profile of v1, /device:TPU:1, one launch (start us, length us, event | category | flops | bytes accessed | tf_op | source)
XLA Modules:
  0.0 113.6 jit_solution(3575449238997220042)
XLA Ops:
  0.6 0.8 reshape.11
  1.5 0.1 broadcast_in_dim.16
  1.6 1.5 %copy.13.w_out_ref = bf16[256,64]{1,0:T(8,128)(2,1)} copy(bf16[256,64]{0,1:T(8,128)(2,1)} %param.10) | data formatting | bytes 65536 | tf_op args[3]
  3.1 0.8 broadcast_in_dim.17.wcol_ref
  3.9 103.7 %shard_map.94 = (f32[64,256]{1,0:T(8,128)}, f32[64,256]{1,0:T(8,128)}, f32[1,128]{1,0:T(1,128)}) custom-call(bf16[64,2,8,1024]{3,2,1,0:T(8,128)(2,1)} %bitcast.5, bf16[2,64,8,256]{3,2,1,0:T(8,128)(2,1)} %target_hbm.1, bf16[64,256]{1,0:T(8,128)(2,1)} %w_in_ref.1, bf16[256,64]{1,0:T(8,128)(2,1)} %copy.13.w_out_ref, bf16[8,256,256]{2,1,0:T(8,128)(2,1)} %leg_hbm.1, ...), custom_call_target="tpu_custom_call" | custom-call | tf_op jit(solution)/shard_map/pallas_call | solution.py:364
  107.6 1.3 %reduce_sum.9 = f32[]{:T(128)} reduce(f32[1,128]{1,0:T(1,128)} %get-tuple-element.6, f32[]{:T(128)} %constant.1.clone.1), dimensions={0,1}, to_apply=%region_0.0 | reduce | flops 127 | bytes 520 | tf_op jit(solution)/shard_map/reduce_sum | solution.py:420
  109.5 1.5 %copy.16 = f32[64,256]{1,0:T(8,128)} copy(f32[64,256]{1,0:T(8,128)} %get-tuple-element.13) | data formatting | bytes 131072
  111.0 1.5 %copy.17 = f32[256,64]{0,1:T(8,128)} copy(f32[256,64]{0,1:T(8,128)} %bitcast.7) | data formatting | bytes 131072
  (2 shorter events, 0.0 us)

commit v2 on v1

v2 whole, which is shorter than its diff:
```python
import functools
import math

import jax
import jax.numpy as jnp
import numpy as np
from jax import lax
from jax.experimental import pallas as pl
from jax.experimental.pallas import tpu as pltpu
from jax.sharding import PartitionSpec as P

MESH = pl.DeviceIdType.MESH
F32 = jnp.float32
BF16 = jnp.bfloat16
XC = 256


def dot(a, b):
    return jnp.dot(a, b, preferred_element_type=F32)


def base_table(nlon, waves):
    cell = np.arange(nlon, dtype=np.int64)[None, :]
    wave = np.arange(waves, dtype=np.int64)[:, None]
    angle = (cell * wave % nlon).astype(np.float32) * np.float32(2.0 * math.pi / nlon)
    both = np.concatenate([np.cos(angle), -np.sin(angle)], axis=0) / np.float32(math.sqrt(nlon))
    return both.astype(jnp.bfloat16)


def kernel(
    nm, nl, state_hbm, target_hbm, w_in_ref, w_out_ref, leg_hbm, base_hbm, wn_ref,
    out_in, out_out, out_loss,
    st_raw, st32, s_cx, base, wcol, wave_t, wave, w_in_bd, w_out_bd, w_pull, hid, slope, fore, gfull,
    hold, sf, rf, rf_a, rf_b, fg_a, fg_b, sg, rg, leg, leg_p, leg_t, tgt, tw, tgt_t, acc32, gb, bs,
    acc_out, acc_in, lsend, lrow1, lsend2, lrow2, ar_s, ar_a, ar_p, ar_b, ar_q, ar_c,
    in_sem, send1, recv1, send2, recv2, ls_sem, lr_sem, as_sem, ar_sem,
):
    member = lax.axis_index("member")
    lat = lax.axis_index("lat")
    half = lax.rem(member, 2)
    base_member = member - half
    ng = 2 * nl
    me = half * nl + lat
    nlon = wave.shape[0]
    cols = wave.shape[1]
    waves = cols // 2
    deg = leg.shape[1]
    nj = leg.shape[2]

    def at64(t):
        return (base_member + t // nl, lax.rem(t, nl))

    c_state = pltpu.make_async_copy(state_hbm, st_raw, in_sem.at[0])
    c_base = pltpu.make_async_copy(base_hbm, base, in_sem.at[1])
    c_leg = pltpu.make_async_copy(leg_hbm.at[pl.ds(half * 4, 4)], leg, in_sem.at[2])
    c_tgt = pltpu.make_async_copy(target_hbm, tgt, in_sem.at[3])
    c_state.start()
    c_base.start()
    c_leg.start()
    c_tgt.start()

    barrier = pltpu.get_barrier_semaphore()

    def greet(d, carry):
        pl.semaphore_signal(barrier, inc=1, device_id=at64(lax.rem(me + d, ng)), device_id_type=MESH)
        return carry

    lax.fori_loop(1, ng, greet, 0)

    def greet_member(d, carry):
        other = lax.rem(base_member + d, nm)
        pl.semaphore_signal(barrier, inc=1, device_id=(other, lat), device_id_type=MESH)
        return carry

    lax.fori_loop(2, nm, greet_member, 0)

    w_in_bd[...] = jnp.zeros_like(w_in_bd)
    w_pull[...] = jnp.zeros_like(w_pull)
    tall = w_out_ref[...].astype(F32)
    wide = jnp.concatenate([tall, tall, tall, tall], axis=0).T
    lane_group = lax.broadcasted_iota(jnp.int32, wide.shape, 1) >> 6
    for g in range(4):
        w_in_bd[64 * g : 64 * g + 64, 256 * g : 256 * g + 256] = w_in_ref[...]
        w_pull[64 * g : 64 * g + 64, 256 * g : 256 * g + 256] = w_out_ref[...]
        w_out_bd[256 * g : 256 * g + 256, :] = jnp.where(lane_group == g, wide, 0.0).astype(BF16)

    rows_of = [
        jnp.broadcast_to(wn_ref[r : r + 1, :].astype(F32), (128, 128)).T for r in range(wn_ref.shape[0])
    ]
    by_owner = jnp.concatenate(rows_of, axis=0).reshape(nl, 8, 128)
    sub = lax.broadcasted_iota(jnp.int32, (nl, 8, 128), 1)
    r2, r4, r6 = (pltpu.roll(by_owner, k, axis=1) for k in (2, 4, 6))
    first = jnp.where(sub < 2, by_owner, jnp.where(sub < 6, r2, r4))
    second = jnp.where(sub < 2, r4, jnp.where(sub < 6, r6, by_owner))
    wcol[: nl * 8] = first.reshape(nl * 8, 128)
    wcol[nl * 8 :] = second.reshape(nl * 8, 128)

    c_state.wait()

    def widen(xt, carry):
        lanes = pl.ds(pl.multiple_of(xt * 128, 128), 128)
        st32[xt] = st_raw[:, :, :, lanes].astype(F32).reshape(st32.shape[1], 128)
        return carry

    lax.fori_loop(0, nlon // 128, widen, 0)

    c_base.wait()
    lb = min(128, waves)
    rb = min(128, cols)

    def order_rows(r, carry):
        rows = pl.ds(pl.multiple_of(r * rb, rb), rb)
        number = wcol[rows, :][:, :lb]
        part = (lax.broadcasted_iota(jnp.int32, (rb, lb), 0) >> 1) & 1
        lane = lax.broadcasted_iota(jnp.int32, (rb, lb), 1)
        blocks = []
        for b in range(cols // lb):
            q, start = b * lb // waves, b * lb % waves
            same = number == (lane + start).astype(F32)
            blocks.append(jnp.where(same & (part == q), 1.0, 0.0))
        pick = jnp.concatenate(blocks, axis=1).astype(BF16)
        wave_t[rows, :] = dot(pick, base[...]).astype(BF16)
        return carry

    lax.fori_loop(0, cols // rb, order_rows, 0)

    spans = ((1, ng // 2), (ng // 2, ng))

    def send_half(tile, hf, src, dst, ssem, rsem):
        def one(d, carry):
            t = lax.rem(me + d, ng)
            pltpu.make_async_remote_copy(
                src_ref=src.at[tile, t], dst_ref=dst.at[tile, me],
                send_sem=ssem.at[2 * tile + hf], recv_sem=rsem.at[tile],
                device_id=at64(t), device_id_type=MESH,
            ).start()
            return carry

        lax.fori_loop(*spans[hf], one, 0)

    def send_tile(tile, src, dst, ssem, rsem):
        send_half(tile, 0, src, dst, ssem, rsem)
        send_half(tile, 1, src, dst, ssem, rsem)
        dst[tile, me] = src[tile, me]

    def wait_bytes(ref, sem):
        pltpu.make_async_copy(ref, ref, sem).wait()

    def left(tile, hf, src, ssem):
        wait_bytes(src.at[tile, pl.ds(0, spans[hf][1] - spans[hf][0])], ssem.at[2 * tile + hf])

    def here(tile, dst, rsem):
        wait_bytes(dst.at[tile, pl.ds(0, ng - 1)], rsem.at[tile])

    out1 = (sf, rf, send1, recv1)
    out2 = (sg, rg, send2, recv2)
    low4 = lax.broadcasted_iota(jnp.int32, (ng, 8, 128), 1) < 4

    def forward(jp, carry):
        def network(xc, inner):
            rows = pl.ds(pl.multiple_of(xc * XC, XC), XC)
            turned = []
            for xt in range(XC // 128):
                tile = xc * (XC // 128) + xt
                parts = [
                    st32[tile, pl.ds(h * 8 + jp * 2 + j2, 64, stride=16), :]
                    for j2 in range(2) for h in range(2)
                ]
                block = jnp.concatenate(parts, axis=0)
                s_cx[jp, :, pl.ds(pl.multiple_of(tile * 128, 128), 128)] = block.astype(BF16)
                turned.append(block.T)
            field = jnp.concatenate(turned, axis=0)
            pre = dot(field.astype(BF16), w_in_bd[...])
            sig = 0.5 + 0.5 * jnp.tanh(0.5 * pre)
            hidden = (pre * sig).astype(BF16)
            hid[jp, rows, :] = hidden
            slope[jp, rows, :] = (sig * (1.0 + pre * (1.0 - sig))).astype(BF16)
            fore[rows, :] = (field + dot(hidden, w_out_bd[...])).astype(BF16)
            return inner

        lax.fori_loop(0, nlon // XC, network, 0)
        modes = dot(wave_t[...], fore[...])
        one, two = modes[:, :128].reshape(ng, 8, 128), modes[:, 128:].reshape(ng, 8, 128)

        @pl.when(jp == 0)
        def _():
            pl.semaphore_wait(barrier, ng - 1 + nm - 2)

        @pl.when(jp < 2)
        def _():
            sf[jp] = jnp.concatenate([one, two], axis=1).astype(BF16)
            send_tile(jp, *out1)

        @pl.when(jp >= 2)
        def _():
            hold[jp - 2, 0] = jnp.where(low4, one, pltpu.roll(two, 4, axis=1))
            hold[jp - 2, 1] = jnp.where(low4, pltpu.roll(one, 4, axis=1), two)

        return carry

    lax.fori_loop(0, 4, forward, 0)
    for ig in range(2):
        sf[2 + ig] = jnp.concatenate([hold[0, ig], hold[1, ig]], axis=1).astype(BF16)
    send_tile(2, *out1)

    c_leg.wait()
    c_tgt.wait()
    col = lax.broadcasted_iota(jnp.int32, (nj, nj), 1)
    row = lax.broadcasted_iota(jnp.int32, (nj, nj), 0)
    from_col = jnp.where(col >= 4 * nl, col - 4 * nl, col)
    wanted = (from_col >> 2) * 8 + (from_col & 3) + jnp.where(col >= 4 * nl, 4, 0)
    perm = jnp.where(row == wanted, 1.0, 0.0).astype(BF16)
    for i in range(4):
        moved = dot(leg[i], perm)
        leg_p[i] = moved.astype(BF16)
        leg_t[i] = moved.T.astype(BF16)
    for b in range(deg // 128):
        tw[b] = tgt[:, :, :, 128 * b : 128 * b + 128].astype(F32).reshape(tw.shape[1], 128)
    for b in range(deg // 128):
        for i in range(8):
            parts = [tw[b, pl.ds(q * 512 + i, 64, stride=8), :] for q in (0, 0, 1, 1)]
            tgt_t[i, 128 * b : 128 * b + 128, :] = jnp.concatenate(parts, axis=0).T.astype(BF16)

    left(1, 0, sf, send1)
    left(1, 1, sf, send1)
    send_half(3, 0, *out1)
    rf[3, me] = sf[3, me]

    def turn_wave(xt, carry):
        start = pl.multiple_of(xt * 128, 128)
        wave[pl.ds(start, 128), :] = wave_t[:, pl.ds(start, 128)].astype(F32).T.astype(BF16)
        return carry

    lax.fori_loop(0, nlon // 128, turn_wave, 0)
    acc_out[...] = jnp.zeros_like(acc_out)
    acc_in[...] = jnp.zeros_like(acc_in)
    left(2, 0, sf, send1)
    send_half(3, 1, *out1)

    for t in range(2):
        here(t, rf, recv1)
        rf_a[:, 16 * t : 16 * t + 16, :] = rf[t].astype(F32)

    own = wcol[pl.ds(pl.multiple_of(me * 8, 8), 8), :].astype(jnp.int32)
    obj = 1.0 / ((nm // 2) * 64)
    nb = 64
    flat_a = rf_a.reshape(ng * 32, 128)
    flat_ga = fg_a.reshape(ng * 32, 128)

    def middle(ig, loss8):
        here(2 + ig, rf, recv1)
        rf_b[ig] = rf[2 + ig].astype(F32)
        flat_b = rf_b.at[ig].reshape(ng * 16, 128)
        flat_gb = fg_b.at[ig].reshape(ng * 16, 128)
        for i2 in range(2):
            for e in range(2):
                early = [
                    flat_a[pl.ds(e * nl * 32 + ig * 4 + q * 2 + i2, nl * 4, stride=8), :] for q in range(2)
                ]
                late = [flat_b[pl.ds(e * nl * 16 + q * 2 + i2, nl * 4, stride=4), :] for q in range(2)]
                modes = jnp.concatenate(
                    [jnp.concatenate(early, axis=1), jnp.concatenate(late, axis=1)], axis=0
                )
                acc32[i2, e] = dot(leg_p[2 * ig + i2], modes.astype(BF16))

        def compare(c, carry):
            rows = pl.ds(pl.multiple_of(c * nb, nb), nb)
            degree = lax.broadcasted_iota(jnp.int32, (nb, 128), 0) + c * nb
            south = lax.broadcasted_iota(jnp.int32, (nb, 128), 1) >= 64
            loss = jnp.zeros((nb, 128), F32)
            for i2 in range(2):
                gap = degree - own[4 * ig + i2 : 4 * ig + i2 + 1, :]
                live = gap >= 0
                sign = jnp.where((gap & 1) == 0, 1.0, -1.0)
                turn = jnp.where(south, sign, 1.0)
                for q in range(2):
                    lanes = slice(128 * q, 128 * q + 128)
                    coeffs = []
                    for e in range(2):
                        part = acc32[i2, e, rows, lanes]
                        whole = part + sign * pltpu.roll(part, 64, axis=1)
                        coeffs.append(jnp.where(live, whole, 0.0).astype(BF16).astype(F32))
                    aim = tgt_t[half * 4 + 2 * ig + i2, rows, lanes].astype(F32) * turn
                    d0, d1, ds = coeffs[0] - aim, coeffs[1] - aim, coeffs[0] - coeffs[1]
                    u0, u1, us = d0 * d0 + 1.0, d1 * d1 + 1.0, ds * ds + 1.0
                    r0, r1, rs = lax.rsqrt(u0), lax.rsqrt(u1), lax.rsqrt(us)
                    term = 0.5 * ((u0 * r0 - 1.0) + (u1 * r1 - 1.0) - (us * rs - 1.0))
                    loss = loss + jnp.where(live, term, 0.0)
                    pull = 0.5 * (ds * rs)
                    gb[i2, 0, rows, lanes] = jnp.where(live, (0.5 * (d0 * r0) - pull) * obj, 0.0).astype(BF16)
                    gb[i2, 1, rows, lanes] = jnp.where(live, (0.5 * (d1 * r1) + pull) * obj, 0.0).astype(BF16)
            return carry + jnp.sum(loss.reshape(nb // 8, 8, 128), axis=0)

        loss8 = lax.fori_loop(0, deg // nb, compare, loss8)
        for i2 in range(2):
            for e in range(2):
                back = dot(leg_t[2 * ig + i2], gb[i2, e])
                for q in range(2):
                    lanes = slice(128 * q, 128 * q + 128)
                    flat_gb[pl.ds(e * nl * 16 + q * 2 + i2, nl * 4, stride=4), :] = back[: nl * 4, lanes]
                    flat_ga[pl.ds(e * nl * 32 + ig * 4 + q * 2 + i2, nl * 4, stride=8), :] = back[nl * 4 :, lanes]
        sg[ig] = fg_b[ig].astype(BF16)
        send_tile(ig, *out2)
        return loss8

    loss8 = middle(0, jnp.zeros((8, 128), F32))
    loss8 = middle(1, loss8)
    for t in range(2):
        sg[2 + t] = fg_a[:, 16 * t : 16 * t + 16, :].astype(BF16)
        rg[2 + t, me] = sg[2 + t, me]

    def to_lats(src_of, dst, ssem, rsem):
        def one(d, carry):
            t = lax.rem(lat + d, nl)
            pltpu.make_async_remote_copy(
                src_ref=src_of(t), dst_ref=dst.at[lat], send_sem=ssem, recv_sem=rsem,
                device_id=(member, t), device_id_type=MESH,
            ).start()
            return carry

        lax.fori_loop(1, nl, one, 0)

    def to_members(src, dst, ssem, rsem):
        def one(d, carry):
            t = lax.rem(member + d, nm)
            pltpu.make_async_remote_copy(
                src_ref=src, dst_ref=dst.at[member], send_sem=ssem, recv_sem=rsem,
                device_id=(t, lat), device_id_type=MESH,
            ).start()
            return carry

        lax.fori_loop(1, nm, one, 0)

    lsend[...] = jnp.sum(loss8, axis=0, keepdims=True)
    to_lats(lambda t: lsend, lrow1, ls_sem.at[0], lr_sem.at[0])
    lrow1[lat] = lsend[...]

    left(0, 0, sg, send2)
    left(0, 1, sg, send2)
    send_half(2, 0, *out2)
    left(1, 0, sg, send2)
    send_half(2, 1, *out2)

    per = 8 // ar_s.shape[2]
    step = ar_s.shape[2]

    def share(k, acc):
        for t in range(16):
            r, c = t // 2, t % 2
            for u in range(per):
                ar_s[k, t * per + u] = acc[8 * r + step * u : 8 * r + step * u + step, 128 * c : 128 * c + 128]
        to_lats(lambda t: ar_s.at[k, t], ar_a.at[k], as_sem.at[3 * k], ar_sem.at[3 * k])
        ar_a[k, lat] = ar_s[k, lat]

    def backward(jp, last=False):
        if jp < 2:
            even = jp * 8
            va = rg[0].astype(F32)[:, even : even + 8]
            vb = rg[1].astype(F32)[:, even : even + 8]
            one = jnp.where(low4, va, pltpu.roll(vb, 4, axis=1))
            two = jnp.where(low4, pltpu.roll(va, 4, axis=1), vb)
        else:
            block = rg[jp].astype(F32)
            one, two = block[:, :8], block[:, 8:]
        bs[:, :128] = one.reshape(cols, 128).astype(BF16)
        bs[:, 128:] = two.reshape(cols, 128).astype(BF16)

        def out_step(xc, inner):
            rows = pl.ds(pl.multiple_of(xc * XC, XC), XC)
            grad = dot(wave[rows, :], bs[...])
            grad16 = grad.astype(BF16)
            gfull[rows, :] = grad16
            turned = grad16.astype(F32).T.astype(BF16)
            total = jnp.zeros((64, 256), F32)
            for g in range(4):
                total = total + dot(turned[64 * g : 64 * g + 64], hid[jp, rows, 256 * g : 256 * g + 256])
            acc_out[...] += total
            return inner

        def in_step(xc, inner):
            rows = pl.ds(pl.multiple_of(xc * XC, XC), XC)
            act = (dot(gfull[rows, :], w_pull[...]) * slope[jp, rows, :].astype(F32)).astype(BF16)
            total = jnp.zeros((64, 256), F32)
            for g in range(4):
                total = total + dot(s_cx[jp, 64 * g : 64 * g + 64, rows], act[:, 256 * g : 256 * g + 256])
            acc_in[...] += total
            return inner

        lax.fori_loop(0, nlon // XC, out_step, 0)
        if last:
            share(0, acc_out)
        lax.fori_loop(0, nlon // XC, in_step, 0)

    here(0, rg, recv2)
    here(1, rg, recv2)
    left(1, 1, sg, send2)
    send_half(3, 0, *out2)
    backward(0)
    left(2, 0, sg, send2)
    send_half(3, 1, *out2)
    backward(1)
    wait_bytes(lrow1.at[pl.ds(0, nl - 1)], lr_sem.at[0])
    lsend2[...] = jnp.sum(lrow1[...], axis=0)
    to_members(lsend2, lrow2, ls_sem.at[1], lr_sem.at[1])
    lrow2[member] = lsend2[...]
    here(2, rg, recv2)
    backward(2)
    here(3, rg, recv2)
    backward(3, True)

    share(1, acc_in)
    for k in range(2):
        wait_bytes(ar_a.at[k, pl.ds(0, nl - 1)], ar_sem.at[3 * k])
        ar_p[k] = jnp.sum(ar_a[k], axis=0)
        to_members(ar_p.at[k], ar_b.at[k], as_sem.at[3 * k + 1], ar_sem.at[3 * k + 1])
        ar_b[k, member] = ar_p[k]
    for k in range(2):
        wait_bytes(ar_b.at[k, pl.ds(0, nm - 1)], ar_sem.at[3 * k + 1])
        ar_q[k] = jnp.sum(ar_b[k], axis=0)
        to_lats(lambda t: ar_q.at[k], ar_c.at[k], as_sem.at[3 * k + 2], ar_sem.at[3 * k + 2])
        ar_c[k, lat] = ar_q[k]
    wait_bytes(lrow2.at[pl.ds(0, nm - 1)], lr_sem.at[1])
    out_loss[...] = jnp.sum(lrow2[...], axis=0)
    for t in range(4):
        for hf in range(2):
            if (t, hf) not in ((1, 0), (1, 1), (2, 0)):
                left(t, hf, sf, send1)
            if (t, hf) not in ((0, 0), (0, 1), (1, 0), (1, 1), (2, 0)):
                left(t, hf, sg, send2)
    wait_bytes(lrow1.at[pl.ds(0, nl - 1)], ls_sem.at[0])
    wait_bytes(lrow2.at[pl.ds(0, nm - 1)], ls_sem.at[1])
    for k, out in ((0, out_out), (1, out_in)):
        wait_bytes(ar_c.at[k, pl.ds(0, nl - 1)], ar_sem.at[3 * k + 2])
        for t in range(16):
            r, c = t // 2, t % 2
            for u in range(per):
                out[8 * r + step * u : 8 * r + step * u + step, 128 * c : 128 * c + 128] = ar_c[k, t * per + u]
    for k in range(2):
        wait_bytes(ar_a.at[k, pl.ds(0, nl - 1)], as_sem.at[3 * k])
        wait_bytes(ar_b.at[k, pl.ds(0, nm - 1)], as_sem.at[3 * k + 1])
        wait_bytes(ar_c.at[k, pl.ds(0, nl - 1)], as_sem.at[3 * k + 2])


def finish(scale, g_in, g_out, loss, o_in, o_out, o_loss):
    o_in[...] = g_in[...]
    o_out[...] = g_out[...]
    o_loss[...] = jnp.sum(loss[...], axis=1, keepdims=True) * scale


def body(nm, nl, state, target, w_in, w_out, legendre, wavenumber_of):
    _, channels, hemis, rows, nlon = state.shape
    slots, deg, nj = legendre.shape
    waves = slots * nl
    cols = 2 * waves
    ng = 2 * nl
    base = jnp.asarray(base_table(nlon, waves))
    vmem = pl.BlockSpec(memory_space=pltpu.VMEM)
    hbm = pl.BlockSpec(memory_space=pl.ANY)
    dma = pltpu.SemaphoreType.DMA
    piece = 128 // nl
    v = pltpu.VMEM
    sums = (
        jax.ShapeDtypeStruct((64, 256), F32),
        jax.ShapeDtypeStruct((64, 256), F32),
        jax.ShapeDtypeStruct((1, 128), F32),
    )
    parts = pl.pallas_call(
        functools.partial(kernel, nm, nl),
        out_shape=sums,
        in_specs=[hbm, hbm, vmem, vmem, hbm, hbm, vmem],
        out_specs=(vmem, vmem, vmem),
        scratch_shapes=[
            v((channels, hemis, rows, nlon), BF16),
            v((nlon // 128, channels * hemis * rows, 128), F32),
            v((4, 256, nlon), BF16),
            v((cols, nlon), BF16),
            v((cols, 128), F32),
            v((cols, nlon), BF16),
            v((nlon, cols), BF16),
            v((256, 1024), BF16),
            v((1024, 256), BF16),
            v((256, 1024), BF16),
            v((4, nlon, 1024), BF16),
            v((4, nlon, 1024), BF16),
            v((nlon, 256), BF16),
            v((nlon, 256), BF16),
            v((2, 2, ng, 8, 128), F32),
            v((4, ng, 16, 128), BF16),
            v((4, ng, 16, 128), BF16),
            v((ng, 32, 128), F32),
            v((2, ng, 16, 128), F32),
            v((ng, 32, 128), F32),
            v((2, ng, 16, 128), F32),
            v((4, ng, 16, 128), BF16),
            v((4, ng, 16, 128), BF16),
            v((4, deg, nj), BF16),
            v((4, deg, nj), BF16),
            v((4, nj, deg), BF16),
            v((2, channels, slots, deg), BF16),
            v((deg // 128, 2 * channels * slots, 128), F32),
            v((8, deg, 256), BF16),
            v((2, 2, deg, 256), F32),
            v((2, 2, deg, 256), BF16),
            v((cols, 256), BF16),
            v((64, 256), F32),
            v((64, 256), F32),
            v((1, 128), F32),
            v((nl, 1, 128), F32),
            v((1, 128), F32),
            v((nm, 1, 128), F32),
            v((2, nl, piece, 128), F32),
            v((2, nl, piece, 128), F32),
            v((2, piece, 128), F32),
            v((2, nm, piece, 128), F32),
            v((2, piece, 128), F32),
            v((2, nl, piece, 128), F32),
            dma((4,)), dma((8,)), dma((4,)), dma((8,)), dma((4,)),
            dma((2,)), dma((2,)), dma((6,)), dma((6,)),
        ],
        compiler_params=pltpu.CompilerParams(
            collective_id=0, has_side_effects=True, vmem_limit_bytes=60 * 1024 * 1024
        ),
    )(state[0], target, w_in, w_out.T, legendre, base, wavenumber_of.reshape(-1, 128))
    scale = 0.5 / ((nm // 2) * channels) / (waves * deg)
    grad_in, grad_out, loss = pl.pallas_call(
        functools.partial(finish, scale),
        out_shape=(sums[0], sums[1], jax.ShapeDtypeStruct((1, 1), F32)),
        in_specs=[vmem, vmem, vmem],
        out_specs=(vmem, vmem, vmem),
    )(*parts)
    return loss.reshape(()), grad_in, grad_out.T


def solution(mesh):
    return jax.shard_map(
        functools.partial(body, mesh.shape["member"], mesh.shape["lat"]),
        mesh=mesh,
        in_specs=(
            P("member", None, None, "lat", None),
            P(None, None, "lat", None),
            P(),
            P(),
            P("lat", None, None),
            P(),
        ),
        out_specs=(P(), P(), P()),
        check_vma=False,
    )
```

time: 114 us -> 98.5 us (0.86)
  Pallas kernels: 104 us -> 97.6 us
  local copies, waits for them, and re-layouts: 6.22 us -> 0 us
  between operations: 2.45 us -> 0.64 us
  other arithmetic: 1.27 us -> 0 us
    pallas_call x1 -> x2, Pallas kernels: 104 us -> 97.6 us  [the longest x1 96.1 us: body(): pl.pallas_call(functools.partial(kernel, nm, nl), out_shape=sums, in_spec...]
    unnamed x3 -> x0, local copies, waits for them, and re-layouts: 4.44 us -> none
    reduce_sum x1 -> x0, other arithmetic: 1.27 us -> none  [body(): return (jnp.sum(loss) * scale, grad_in, grad_out.T)]
where the time goes in v2:
time: 98.5 us; the launch traced here: 98.3 us
  Pallas kernels  97.6 us (99%)
    pallas_call x1, Pallas kernels, body(): pl.pallas_call(functools.partial(kernel, nm, nl), out_shape=sums, in_spec...  96.1 us

profile of v2, /device:TPU:1, one launch (start us, length us, event | category | flops | bytes accessed | tf_op | source)
XLA Modules:
  0.0 98.3 jit_solution(10361862339768437604)
XLA Ops:
  0.6 96.1 %shard_map.94 = (f32[64,256]{1,0:T(8,128)}, f32[64,256]{1,0:T(8,128)}, f32[1,128]{1,0:T(1,128)}) custom-call(bf16[64,2,8,1024]{3,2,1,0:T(8,128)(2,1)} %bitcast.5, bf16[2,64,8,256]{3,2,1,0:T(8,128)(2,1)} %target_hbm.1, bf16[64,256]{1,0:T(8,128)(2,1)} %w_in_ref.1, bf16[64,256]{1,0:T(8,128)(2,1)} %bitcast.6, bf16[8,256,256]{2,1,0:T(8,128)(2,1)} %leg_hbm.1, ...), custom_call_target="tpu_custom_call" | custom-call | tf_op jit(solution)/shard_map/pallas_call | solution.py:467
  96.7 1.5 %shard_map.95 = (f32[64,256]{1,0:T(8,128)}, f32[64,256]{1,0:T(8,128)}, f32[1,1]{1,0:T(1,128)}) custom-call(f32[64,256]{1,0:T(8,128)} %get-tuple-element.9.g_in, f32[64,256]{1,0:T(8,128)} %get-tuple-element.10.g_out, f32[1,128]{1,0:T(1,128)} %get-tuple-element.11.loss), custom_call_target="tpu_custom_call" | custom-call | tf_op jit(solution)/shard_map/pallas_call | solution.py:525

commit v3 on v2

--- a/solution.py
+++ b/solution.py
@@ -12,7 +12,7 @@
 MESH = pl.DeviceIdType.MESH
 F32 = jnp.float32
 BF16 = jnp.bfloat16
-XC = 256
+XC = 1024
 
 
 def dot(a, b):
@@ -47,8 +47,54 @@
     deg = leg.shape[1]
     nj = leg.shape[2]
 
-    def at64(t):
-        return (base_member + t // nl, lax.rem(t, nl))
+    ny, nz = nl // 4, nm // 2
+    my_core, my_y, my_x, my_z = lax.rem(lat, 2), lax.rem(lat // 2, ny), lat // (2 * ny), member // 2
+    members = (member, base_member + 1 - half)
+    halves = (half, 1 - half)
+    beside = [[x * 2 * ny + c for c in (my_core, 1 - my_core)] for x in (my_x, 1 - my_x)]
+
+    def ring(i, size):
+        return size // 2 + (1 - 2 * lax.rem(i, 2)) * ((i + 1) // 2)
+
+    def wrap(v, size):
+        return jnp.where(v >= size, v - size, v)
+
+    def around(size, lo, hi, act):
+        if hi > lo:
+            lax.fori_loop(lo, min(hi, size - 1), lambda i, carry: (act(i, False), carry)[1], 0)
+        if hi == size:
+            act(size - 1, True)
+
+    def group_step(act):
+        def at(i, stay):
+            y = wrap(my_y + ring(i, ny), ny) * 2
+            for h in range(2):
+                for x in range(2):
+                    for c in range(2):
+                        if not (stay and h == x == c == 0):
+                            there = beside[x][c] + y
+                            act((members[h], there), halves[h] * nl + there)
+
+        return at
+
+    def lat_step(act):
+        def at(i, stay):
+            y = wrap(my_y + ring(i, ny), ny) * 2
+            for x in range(2):
+                for c in range(2):
+                    if not (stay and x == c == 0):
+                        act(beside[x][c] + y)
+
+        return at
+
+    def member_step(act):
+        def at(i, stay):
+            z = wrap(my_z + ring(i, nz), nz) * 2
+            for h in range(2):
+                if not (stay and h == 0):
+                    act(z + halves[h])
+
+        return at
 
     c_state = pltpu.make_async_copy(state_hbm, st_raw, in_sem.at[0])
     c_base = pltpu.make_async_copy(base_hbm, base, in_sem.at[1])
@@ -61,18 +107,13 @@
 
     barrier = pltpu.get_barrier_semaphore()
 
-    def greet(d, carry):
-        pl.semaphore_signal(barrier, inc=1, device_id=at64(lax.rem(me + d, ng)), device_id_type=MESH)
-        return carry
-
-    lax.fori_loop(1, ng, greet, 0)
-
-    def greet_member(d, carry):
-        other = lax.rem(base_member + d, nm)
-        pl.semaphore_signal(barrier, inc=1, device_id=(other, lat), device_id_type=MESH)
-        return carry
-
-    lax.fori_loop(2, nm, greet_member, 0)
+    def greet(there):
+        pl.semaphore_signal(barrier, inc=1, device_id=there, device_id_type=MESH)
+
+    around(ny, 0, ny, group_step(lambda there, t: greet(there)))
+    for d in range(1, nz):
+        for h in range(2):
+            greet((wrap(my_z + d, nz) * 2 + h, lat))
 
     w_in_bd[...] = jnp.zeros_like(w_in_bd)
     w_pull[...] = jnp.zeros_like(w_pull)
@@ -124,19 +165,18 @@
 
     lax.fori_loop(0, cols // rb, order_rows, 0)
 
-    spans = ((1, ng // 2), (ng // 2, ng))
+    spans = ((0, ny // 2), (ny // 2, ny))
+    counts = (ng // 2, ng // 2 - 1)
 
     def send_half(tile, hf, src, dst, ssem, rsem):
-        def one(d, carry):
-            t = lax.rem(me + d, ng)
+        def one(there, t):
             pltpu.make_async_remote_copy(
                 src_ref=src.at[tile, t], dst_ref=dst.at[tile, me],
                 send_sem=ssem.at[2 * tile + hf], recv_sem=rsem.at[tile],
-                device_id=at64(t), device_id_type=MESH,
+                device_id=there, device_id_type=MESH,
             ).start()
-            return carry
-
-        lax.fori_loop(*spans[hf], one, 0)
+
+        around(ny, *spans[hf], group_step(one))
 
     def send_tile(tile, src, dst, ssem, rsem):
         send_half(tile, 0, src, dst, ssem, rsem)
@@ -147,7 +187,7 @@
         pltpu.make_async_copy(ref, ref, sem).wait()
 
     def left(tile, hf, src, ssem):
-        wait_bytes(src.at[tile, pl.ds(0, spans[hf][1] - spans[hf][0])], ssem.at[2 * tile + hf])
+        wait_bytes(src.at[tile, pl.ds(0, counts[hf])], ssem.at[2 * tile + hf])
 
     def here(tile, dst, rsem):
         wait_bytes(dst.at[tile, pl.ds(0, ng - 1)], rsem.at[tile])
@@ -310,26 +350,22 @@
         rg[2 + t, me] = sg[2 + t, me]
 
     def to_lats(src_of, dst, ssem, rsem):
-        def one(d, carry):
-            t = lax.rem(lat + d, nl)
+        def one(t):
             pltpu.make_async_remote_copy(
                 src_ref=src_of(t), dst_ref=dst.at[lat], send_sem=ssem, recv_sem=rsem,
                 device_id=(member, t), device_id_type=MESH,
             ).start()
-            return carry
-
-        lax.fori_loop(1, nl, one, 0)
+
+        around(ny, 0, ny, lat_step(one))
 
     def to_members(src, dst, ssem, rsem):
-        def one(d, carry):
-            t = lax.rem(member + d, nm)
+        def one(t):
             pltpu.make_async_remote_copy(
                 src_ref=src, dst_ref=dst.at[member], send_sem=ssem, recv_sem=rsem,
                 device_id=(t, lat), device_id_type=MESH,
             ).start()
-            return carry
-
-        lax.fori_loop(1, nm, one, 0)
+
+        around(nz, 0, nz, member_step(one))
 
     lsend[...] = jnp.sum(loss8, axis=0, keepdims=True)
     to_lats(lambda t: lsend, lrow1, ls_sem.at[0], lr_sem.at[0])
@@ -341,16 +377,37 @@
     left(1, 0, sg, send2)
     send_half(2, 1, *out2)
 
-    per = 8 // ar_s.shape[2]
-    step = ar_s.shape[2]
+    chips = nl // 2
+    tiles = 16 // chips
 
     def share(k, acc):
         for t in range(16):
             r, c = t // 2, t % 2
-            for u in range(per):
-                ar_s[k, t * per + u] = acc[8 * r + step * u : 8 * r + step * u + step, 128 * c : 128 * c + 128]
-        to_lats(lambda t: ar_s.at[k, t], ar_a.at[k], as_sem.at[3 * k], ar_sem.at[3 * k])
-        ar_a[k, lat] = ar_s[k, lat]
+            u = t % tiles
+            ar_s[k, t // tiles, 8 * u : 8 * u + 8, :] = acc[8 * r : 8 * r + 8, 128 * c : 128 * c + 128]
+
+        def one(chip):
+            pltpu.make_async_remote_copy(
+                src_ref=ar_s.at[k, chip], dst_ref=ar_a.at[lat], send_sem=as_sem.at[0], recv_sem=ar_sem.at[0],
+                device_id=(member, chip * 2 + k), device_id_type=MESH,
+            ).start()
+
+        def at(i, stay):
+            y = wrap(my_y + ring(i, ny), ny)
+            one((1 - my_x) * ny + y)
+            if not stay:
+                one(my_x * ny + y)
+
+        around(ny, 0, ny, at)
+        home = lat // 2
+
+        @pl.when(my_core == k)
+        def _():
+            ar_a[lat] = ar_s[k, home]
+
+        @pl.when(my_core != k)
+        def _():
+            one(home)
 
     def backward(jp, last=False):
         if jp < 2:
@@ -409,16 +466,14 @@
     backward(3, True)
 
     share(1, acc_in)
-    for k in range(2):
-        wait_bytes(ar_a.at[k, pl.ds(0, nl - 1)], ar_sem.at[3 * k])
-        ar_p[k] = jnp.sum(ar_a[k], axis=0)
-        to_members(ar_p.at[k], ar_b.at[k], as_sem.at[3 * k + 1], ar_sem.at[3 * k + 1])
-        ar_b[k, member] = ar_p[k]
-    for k in range(2):
-        wait_bytes(ar_b.at[k, pl.ds(0, nm - 1)], ar_sem.at[3 * k + 1])
-        ar_q[k] = jnp.sum(ar_b[k], axis=0)
-        to_lats(lambda t: ar_q.at[k], ar_c.at[k], as_sem.at[3 * k + 2], ar_sem.at[3 * k + 2])
-        ar_c[k, lat] = ar_q[k]
+    wait_bytes(ar_a.at[pl.ds(0, nl - 1)], ar_sem.at[0])
+    ar_p[...] = jnp.sum(ar_a[...], axis=0)
+    to_members(ar_p, ar_b, as_sem.at[1], ar_sem.at[1])
+    ar_b[member] = ar_p[...]
+    wait_bytes(ar_b.at[pl.ds(0, nm - 1)], ar_sem.at[1])
+    ar_q[...] = jnp.sum(ar_b[...], axis=0)
+    to_lats(lambda t: ar_q, ar_c, as_sem.at[2], ar_sem.at[2])
+    ar_c[lat] = ar_q[...]
     wait_bytes(lrow2.at[pl.ds(0, nm - 1)], lr_sem.at[1])
     out_loss[...] = jnp.sum(lrow2[...], axis=0)
     for t in range(4):
@@ -429,16 +484,15 @@
                 left(t, hf, sg, send2)
     wait_bytes(lrow1.at[pl.ds(0, nl - 1)], ls_sem.at[0])
     wait_bytes(lrow2.at[pl.ds(0, nm - 1)], ls_sem.at[1])
+    wait_bytes(ar_a.at[pl.ds(0, nl - 1)], as_sem.at[0])
+    wait_bytes(ar_b.at[pl.ds(0, nm - 1)], as_sem.at[1])
+    wait_bytes(ar_c.at[pl.ds(0, nl - 1)], ar_sem.at[2])
     for k, out in ((0, out_out), (1, out_in)):
-        wait_bytes(ar_c.at[k, pl.ds(0, nl - 1)], ar_sem.at[3 * k + 2])
         for t in range(16):
             r, c = t // 2, t % 2
-            for u in range(per):
-                out[8 * r + step * u : 8 * r + step * u + step, 128 * c : 128 * c + 128] = ar_c[k, t * per + u]
-    for k in range(2):
-        wait_bytes(ar_a.at[k, pl.ds(0, nl - 1)], as_sem.at[3 * k])
-        wait_bytes(ar_b.at[k, pl.ds(0, nm - 1)], as_sem.at[3 * k + 1])
-        wait_bytes(ar_c.at[k, pl.ds(0, nl - 1)], as_sem.at[3 * k + 2])
+            u = t % tiles
+            out[8 * r : 8 * r + 8, 128 * c : 128 * c + 128] = ar_c[2 * (t // tiles) + k, 8 * u : 8 * u + 8, :]
+    wait_bytes(ar_c.at[pl.ds(0, nl - 1)], as_sem.at[2])
 
 
 def finish(scale, g_in, g_out, loss, o_in, o_out, o_loss):
@@ -457,7 +511,7 @@
     vmem = pl.BlockSpec(memory_space=pltpu.VMEM)
     hbm = pl.BlockSpec(memory_space=pl.ANY)
     dma = pltpu.SemaphoreType.DMA
-    piece = 128 // nl
+    piece = 8 * (32 // nl)
     v = pltpu.VMEM
     sums = (
         jax.ShapeDtypeStruct((64, 256), F32),
@@ -508,14 +562,14 @@
             v((nl, 1, 128), F32),
             v((1, 128), F32),
             v((nm, 1, 128), F32),
-            v((2, nl, piece, 128), F32),
-            v((2, nl, piece, 128), F32),
-            v((2, piece, 128), F32),
-            v((2, nm, piece, 128), F32),
-            v((2, piece, 128), F32),
-            v((2, nl, piece, 128), F32),
+            v((2, nl // 2, piece, 128), F32),
+            v((nl, piece, 128), F32),
+            v((piece, 128), F32),
+            v((nm, piece, 128), F32),
+            v((piece, 128), F32),
+            v((nl, piece, 128), F32),
             dma((4,)), dma((8,)), dma((4,)), dma((8,)), dma((4,)),
-            dma((2,)), dma((2,)), dma((6,)), dma((6,)),
+            dma((2,)), dma((2,)), dma((3,)), dma((3,)),
         ],
         compiler_params=pltpu.CompilerParams(
             collective_id=0, has_side_effects=True, vmem_limit_bytes=60 * 1024 * 1024

time: 98.5 us -> 90.1 us (0.915)
  Pallas kernels: 97.6 us -> 89.2 us
    pallas_call x1, Pallas kernels: 96.1 us -> 87.7 us  [body(): pl.pallas_call(functools.partial(kernel, nm, nl), out_shape=sums, in_spec...]
where the time goes in v3:
time: 90.1 us; the launch traced here: 89.8 us
  Pallas kernels  89.2 us (99%)
    pallas_call x1, Pallas kernels, body(): pl.pallas_call(functools.partial(kernel, nm, nl), out_shape=sums, in_spec...  87.7 us

profile of v3, /device:TPU:1, one launch (start us, length us, event | category | flops | bytes accessed | tf_op | source)
XLA Modules:
  0.0 89.8 jit_solution(126090980566348525)
XLA Ops:
  0.6 87.7 %shard_map.94 = (f32[64,256]{1,0:T(8,128)}, f32[64,256]{1,0:T(8,128)}, f32[1,128]{1,0:T(1,128)}) custom-call(bf16[64,2,8,1024]{3,2,1,0:T(8,128)(2,1)} %bitcast.5, bf16[2,64,8,256]{3,2,1,0:T(8,128)(2,1)} %target_hbm.1, bf16[64,256]{1,0:T(8,128)(2,1)} %w_in_ref.1, bf16[64,256]{1,0:T(8,128)(2,1)} %bitcast.6, bf16[8,256,256]{2,1,0:T(8,128)(2,1)} %leg_hbm.1, ...), custom_call_target="tpu_custom_call" | custom-call | tf_op jit(solution)/shard_map/pallas_call | solution.py:521
  88.3 1.5 %shard_map.95 = (f32[64,256]{1,0:T(8,128)}, f32[64,256]{1,0:T(8,128)}, f32[1,1]{1,0:T(1,128)}) custom-call(f32[64,256]{1,0:T(8,128)} %get-tuple-element.9.g_in, f32[64,256]{1,0:T(8,128)} %get-tuple-element.10.g_out, f32[1,128]{1,0:T(1,128)} %get-tuple-element.11.loss), custom_call_target="tpu_custom_call" | custom-call | tf_op jit(solution)/shard_map/pallas_call | solution.py:579

commit v4 on v3

--- a/solution.py
+++ b/solution.py
@@ -61,7 +61,7 @@
 
     def around(size, lo, hi, act):
         if hi > lo:
-            lax.fori_loop(lo, min(hi, size - 1), lambda i, carry: (act(i, False), carry)[1], 0)
+            lax.fori_loop(lo, min(hi, size - 1), lambda i, carry: (act(i, False), carry)[1], 0, unroll=True)
         if hi == size:
             act(size - 1, True)
 
@@ -80,7 +80,7 @@
     def lat_step(act):
         def at(i, stay):
             y = wrap(my_y + ring(i, ny), ny) * 2
-            for x in range(2):
+            for x in (1, 0):
                 for c in range(2):
                     if not (stay and x == c == 0):
                         act(beside[x][c] + y)
@@ -90,7 +90,7 @@
     def member_step(act):
         def at(i, stay):
             z = wrap(my_z + ring(i, nz), nz) * 2
-            for h in range(2):
+            for h in (1, 0):
                 if not (stay and h == 0):
                     act(z + halves[h])
 
@@ -100,8 +100,8 @@
     c_base = pltpu.make_async_copy(base_hbm, base, in_sem.at[1])
     c_leg = pltpu.make_async_copy(leg_hbm.at[pl.ds(half * 4, 4)], leg, in_sem.at[2])
     c_tgt = pltpu.make_async_copy(target_hbm, tgt, in_sem.at[3])
+    c_base.start()
     c_state.start()
-    c_base.start()
     c_leg.start()
     c_tgt.start()
 
@@ -135,15 +135,6 @@
     second = jnp.where(sub < 2, r4, jnp.where(sub < 6, r6, by_owner))
     wcol[: nl * 8] = first.reshape(nl * 8, 128)
     wcol[nl * 8 :] = second.reshape(nl * 8, 128)
-
-    c_state.wait()
-
-    def widen(xt, carry):
-        lanes = pl.ds(pl.multiple_of(xt * 128, 128), 128)
-        st32[xt] = st_raw[:, :, :, lanes].astype(F32).reshape(st32.shape[1], 128)
-        return carry
-
-    lax.fori_loop(0, nlon // 128, widen, 0)
 
     c_base.wait()
     lb = min(128, waves)
@@ -164,6 +155,15 @@
         return carry
 
     lax.fori_loop(0, cols // rb, order_rows, 0)
+
+    c_state.wait()
+
+    def widen(xt, carry):
+        lanes = pl.ds(pl.multiple_of(xt * 128, 128), 128)
+        st32[xt] = st_raw[:, :, :, lanes].astype(F32).reshape(st32.shape[1], 128)
+        return carry
+
+    lax.fori_loop(0, nlon // 128, widen, 0)
 
     spans = ((0, ny // 2), (ny // 2, ny))
     counts = (ng // 2, ng // 2 - 1)
@@ -283,7 +283,7 @@
 
     own = wcol[pl.ds(pl.multiple_of(me * 8, 8), 8), :].astype(jnp.int32)
     obj = 1.0 / ((nm // 2) * 64)
-    nb = 64
+    nb = 128
     flat_a = rf_a.reshape(ng * 32, 128)
     flat_ga = fg_a.reshape(ng * 32, 128)
 

time: 90.1 us -> 89.6 us (level)
  no operation moved by 1% of the time
where the time goes in v4:
time: 89.6 us; the launch traced here: 89.3 us
  Pallas kernels  88.7 us (99%)
    pallas_call x1, Pallas kernels, body(): pl.pallas_call(functools.partial(kernel, nm, nl), out_shape=sums, in_spec...  87.2 us

profile of v4, /device:TPU:1, one launch (start us, length us, event | category | flops | bytes accessed | tf_op | source)
XLA Modules:
  0.0 89.3 jit_solution(851103940710026361)
XLA Ops:
  0.6 87.2 %shard_map.94 = (f32[64,256]{1,0:T(8,128)}, f32[64,256]{1,0:T(8,128)}, f32[1,128]{1,0:T(1,128)}) custom-call(bf16[64,2,8,1024]{3,2,1,0:T(8,128)(2,1)} %bitcast.5, bf16[2,64,8,256]{3,2,1,0:T(8,128)(2,1)} %target_hbm.1, bf16[64,256]{1,0:T(8,128)(2,1)} %w_in_ref.1, bf16[64,256]{1,0:T(8,128)(2,1)} %bitcast.6, bf16[8,256,256]{2,1,0:T(8,128)(2,1)} %leg_hbm.1, ...), custom_call_target="tpu_custom_call" | custom-call | tf_op jit(solution)/shard_map/pallas_call | solution.py:521
  87.8 1.5 %shard_map.95 = (f32[64,256]{1,0:T(8,128)}, f32[64,256]{1,0:T(8,128)}, f32[1,1]{1,0:T(1,128)}) custom-call(f32[64,256]{1,0:T(8,128)} %get-tuple-element.9.g_in, f32[64,256]{1,0:T(8,128)} %get-tuple-element.10.g_out, f32[1,128]{1,0:T(1,128)} %get-tuple-element.11.loss), custom_call_target="tpu_custom_call" | custom-call | tf_op jit(solution)/shard_map/pallas_call | solution.py:579
